TPU v7x, 32 devices: a whole 2x2x4 slice. The times are simulated.
32 devices in a mesh: grp: 2 (over x), row: 16 (over z, y, core).
Axes of the slice: x: 2, y: 2, z: 4, core: 2. Of those that a mesh axis runs over, the one named last changes fastest.
Arguments:
- populations: float32 [32768, 512], P(('grp', 'row')), parts along dimension 0
- rate_blocks: float32 [256, 6, 2, 128, 128], P(('grp', 'row')), parts along dimension 0
- columns: int32 [256, 6, 2], P(('grp', 'row')), parts along dimension 0, may hold values from 0 to 7
- counts: int32 [256, 6], P(('grp', 'row')), parts along dimension 0, may hold values from 0 to 2, as said below
- owners: int32 [6], replicated, may hold values from 0 to 15, as said below
Outputs:
- krylov_basis: float32 [32768, 512], P(('grp', 'row')), parts along dimension 0
- chain_scale: float32 [1024], P('grp'), parts along dimension 0
There are 2 independent parts, one for each index of `grp`. A program takes and returns all parts, laid end to end along the dimension named above; an argument that names none is the same for every part. Nothing has to cross between parts.
Inputs may be any that keep to these rules, and one draw needn't show every extreme that they name: `owners`: distinct devices of the row axis. `counts`: in every panel some block row has 2 live slots.
All inputs are finite; a program needn't handle non-finite values.
Results may differ from a plain program's by a relative error of at most 0.0001.
Values sent between devices are 32-bit elements; how exact they have to be, the bound alone decides.
A program may use at most 128 MiB of HBM per device.

v0:
```python
import jax
import jax.numpy as jnp
from jax import lax
from jax.sharding import PartitionSpec as P


def spread(block, axis, holder):
    block = jnp.where(lax.axis_index(axis) == holder, block, jnp.zeros_like(block))
    return lax.psum(block, axis)


def on_device(populations, rate_blocks, columns, counts, owners):
    block_rows, panels, slot_count, block_size, unused_size = rate_blocks.shape
    chains = populations.shape[1]
    running = jnp.zeros((block_rows, block_size, chains), jnp.float32)
    for k in range(panels):
        panel_rows = spread(populations, "row", owners[k])
        contribute_running = running
        contribute_panel_blocks = panel_rows.reshape(block_rows, block_size, chains)
        for contribute_s in range(slot_count):
            picked = contribute_panel_blocks[columns[:, k, contribute_s]]
            live_mask = (contribute_s < counts[:, k]).astype(jnp.float32)
            weight = rate_blocks[:, k, contribute_s] * live_mask[:, None, None]
            contribute_running = contribute_running + jnp.einsum(
                "rij,rjc->ric", weight, picked, precision=lax.Precision.HIGHEST
            )
        running = contribute_running
    product = running.reshape(block_rows * block_size, chains)
    squares = jnp.sum(product * product, axis=0)
    total_squares = lax.psum(squares, "row")
    levels = product.shape[0] * lax.axis_size("row")
    chain_scale = jnp.sqrt(total_squares / levels + 1e-06)
    return (product / chain_scale, chain_scale)


def solution(mesh):
    in_specs = (
        P(("grp", "row"), None),
        P(("grp", "row"), None, None, None, None),
        P(("grp", "row"), None, None),
        P(("grp", "row"), None),
        P(),
    )
    out_specs = (P(("grp", "row"), None), P("grp"))
    return jax.shard_map(
        on_device, mesh=mesh, in_specs=in_specs, out_specs=out_specs, check_vma=False
    )
```

profile of v0, /device:TPU:0, one launch (start us, length us, event | category | flops | bytes accessed | tf_op | source)
XLA Modules:
  0.0 383.7 jit_solution(4369193330786929281)
XLA Ops:
  7.2 0.0 all-reduce.3.cloned.1.call-start
  7.2 1.6 fusion.60
  12.6 6.5 %broadcast_select_fusion.5 = (f32[1024,512]{1,0:T(8,128)}, f32[1024,512]{1,0:T(8,128)}, f32[1024,512]{1,0:T(8,128)}, f32[1024,512]{1,0:T(8,128)}, f32[1024,512]{1,0:T(8,128)}, /*index=5*/f32[1024,512]{1,0:T(8,128)}) fusion(f32[1024,512]{1,0:T(8,128)} %param.5, pred[]{:T(512)S(6)} %eq.18, pred[]{:T(512)S(6)} %eq.21, pred[]{:T(512)S(6)} %eq.20, pred[]{:T(512)S(6)} %eq.19, ...), kind=kLoop, calls=%fused_computation.20 | loop fusion | flops 3145728 | bytes 14680070 | tf_op jit(solution)/shard_map/jit(_where)/select_n | solution.py:8
  19.1 0.0 all-reduce.3.cloned.1.call-update
  19.1 0.7 copy-done.10
  19.8 0.1 fusion.59
  19.9 0.1 copy.13
  19.9 0.1 copy.17
  20.0 0.1 copy.16
  20.1 0.1 copy.15
  20.2 0.1 copy.14
  20.3 0.1 copy.18
  20.3 0.0 copy-done.12
  20.5 238.0 %all-reduce.3.cloned.1.call-done = (f32[8,128,512]{2,1,0:T(8,128)}, f32[8,128,512]{2,1,0:T(8,128)}, f32[8,128,512]{2,1,0:T(8,128)}, f32[8,128,512]{2,1,0:T(8,128...) async-done(((f32[8,128,512]{2,1,0:T(8,128)}, f32[8,128,512]{2,1,0:T(8,128)}, f32[8,128,512]{2,1,0:T(8,128)}, f32[8,128,512]{2,1,0:T(8,128)}, f32[8,128,512]{2,1,0:T(8,128)}, ...) | async-done | bytes 12582928 | tf_op jit(solution)/shard_map/psum | solution.py:9
  258.6 2.3 gather_fusion.11
  260.8 3.6 gather_fusion.10
  264.4 3.7 gather_fusion.9
  268.1 3.6 gather_fusion.8
  271.7 3.6 gather_fusion.7
  275.3 3.6 gather_fusion.6
  278.9 3.7 gather_fusion.5
  282.5 3.6 gather_fusion.4
  286.1 3.6 gather_fusion.3
  289.8 3.6 gather_fusion.2
  293.3 3.6 gather_fusion.1
  296.9 3.6 gather_fusion
  300.5 3.9 %fusion = f32[8,128,512]{2,1,0:T(8,128)S(1)} fusion(f32[8,128,512]{2,1,0:T(8,128)} %gather_fusion.10, f32[8,6,2,128,128]{4,3,2,1,0:T(8,128)} %param.6, f32[8]{0:T(128)S(1)} %get-tuple-element.33), kind=kOutput, calls=%fused_computation.23 | convolution fusion | flops 805437440 | bytes 4718624 | tf_op jit(solution)/shard_map/rij,rjc->ric/dot_general | solution.py:24
  304.4 3.2 fusion.2
  307.6 3.2 fusion.1
  310.8 0.0 copy-done.8
  310.8 0.0 copy-start.3
  310.8 3.2 fusion.4
  314.0 3.4 fusion.3
  317.4 0.0 copy-done.7
  317.4 0.0 copy-start.2
  317.4 3.2 fusion.6
  320.6 3.2 fusion.5
  323.8 0.0 copy-done.5
  323.8 0.0 copy-start
  323.8 3.2 fusion.8
  327.0 0.0 copy-done
  327.0 0.0 copy-start.6
  327.0 3.2 fusion.7
  330.2 3.2 fusion.10
  333.4 3.1 fusion.9
  336.4 5.4 %multiply_reduce_fusion = (f32[512]{0:T(512)S(1)}, f32[8,128,512]{2,1,0:T(8,128)}) fusion(f32[8,128,512]{2,1,0:T(8,128)S(1)} %gather_fusion.11, f32[8,6,2,128,128]{4,3,2,1,0:T(8,128)} %param.6, f32[8]{0:T(128)S(1)} %get-tuple-element.32, f32[8,128,512]{2,1,0:T(8,128)S(1)} %fusion, f32[8,128,512]{2,1,0:T(8,128)S(1)} %fusion.1, ...), kind=kOutput, calls=%fused_computation.13 | convolution fusion | flops 812252672 | bytes 27789344 | tf_op jit(solution)/shard_map/rij,rjc->ric/dot_general | solution.py:24
  341.9 31.8 %psum.55 = f32[512]{0:T(512)S(1)} all-reduce(f32[512]{0:T(512)S(1)} %get-tuple-element.50), channel_id=1, replica_groups=mesh['grp'=2,'row'=16] {'row'}, use_global_device_ids=true, to_apply=%region_7.8 | all-reduce | flops 512 | bytes 4096 | tf_op jit(solution)/shard_map/psum | solution.py:30
  373.6 3.2 bitcast_divide_fusion
  (30 shorter events, 0.1 us)
Async XLA Ops:
  7.2 251.4 %all-reduce.3.cloned.1.call-start = ((), (), s32[]{:S(2)}) async-start(), calls=%async_computation | async-start | bytes 25165824 | tf_op jit(solution)/shard_map/psum | solution.py:9
  19.1 0.7 copy-start.10
  19.1 1.2 copy-start.12
  300.5 3.9 %copy-start.9 = (f32[8,128,512]{2,1,0:T(8,128)S(1)}, f32[8,128,512]{2,1,0:T(8,128)}, u32[]{:S(2)}) copy-start(f32[8,128,512]{2,1,0:T(8,128)} %gather_fusion.8) | copy-start | bytes 6291460
  304.4 3.2 copy-start.4
  307.6 3.2 copy-start.8
  310.8 3.2 copy-start.3
  314.0 3.4 copy-start.7
  317.4 3.2 copy-start.2
  320.6 3.2 copy-start.5
  323.8 3.2 copy-start
  327.0 3.2 copy-start.6
  330.2 3.2 copy-start.1
  373.6 3.2 copy-start.11
Sparse Core Ops, SparseCore 0:
  19.2 239.2 all-reduce.2
where the time goes:
time: 385 us; the launch traced here: 384 us
  waiting for transfers between devices  238 us (62%)
  local copies, waits for them, and re-layouts  44.8 us (12%)
  matrix products  41.1 us (11%)
  blocking collectives  31.8 us (8%)
  between operations  18.3 us (5%)
  other arithmetic  9.74 us (3%)
    psum x1, waiting for transfers between devices, spread(): return lax.psum(block, axis)  238 us
    gather x12, local copies, waits for them, and re-layouts, on_device(): picked = contribute_panel_blocks[columns[:, k, contribute_s]]  42 us
    dot_general x12, matrix products, on_device(): jnp.einsum('rij,rjc->ric', weight, picked, precision=lax.Precision.HIGHEST)  41.1 us
    psum x1, blocking collectives, on_device(): total_squares = lax.psum(squares, 'row')  31.8 us
  transfers between devices with their start and end apart: 1, of which 1 were waited for; matrix products, arithmetic and copies ran while one was open for 0% of the time, Pallas kernels for 0%

commit v1 on v0

v1 whole, which is shorter than its diff:
```python
import functools

import jax
import jax.numpy as jnp
from jax import lax
from jax.experimental import pallas as pl
from jax.experimental.pallas import tpu as pltpu
from jax.sharding import PartitionSpec as P

CHUNKS = 4
SKEW = 2
LAG_Y = 2
LAG_C = 1
MESH = pl.DeviceIdType.MESH


def grid_of(devices):
    pairs = devices // 2
    nb = 1
    while (nb * 2) * (nb * 2) <= pairs:
        nb *= 2
    return pairs // nb, nb


def split(x):
    high = x.astype(jnp.bfloat16)
    low = (x - high.astype(jnp.float32)).astype(jnp.bfloat16)
    return high, low


def kernel(na, nb, chunks, panels, pop, rates, columns, counts, owners, product, squares,
           weight_f32, weights, y_in, core_in, plane, up, down, full, high, low, acc,
           sum_mine, sum_y, sum_core, sum_a, weight_sem,
           yp_s, yp_r, cp_s, cp_r, up_s, up_r, dn_s, dn_r, yq_s, yq_r, cq_s, cq_r,
           sy_s, sy_r, sc_s, sc_r, sa_s, sa_r):
    me = lax.axis_index("row")
    core = lax.rem(me, 2)
    b = lax.rem(me // 2, nb)
    a = me // (2 * nb)
    other = 1 - core
    units = chunks * panels
    width = pop.shape[3] // chunks
    block_rows, block_size = product.shape[0], product.shape[1]

    def at(a_, b_, core_):
        return {"row": (a_ * nb + b_) * 2 + core_}

    def b_plus(d):
        return lax.rem(b + d, nb)

    def b_minus(d):
        return lax.rem(b + nb - d, nb)

    def remote(src, dst, send, recv, where):
        return pltpu.make_async_remote_copy(
            src_ref=src, dst_ref=dst, send_sem=send, recv_sem=recv,
            device_id=where, device_id_type=MESH)

    load_weights = pltpu.make_async_copy(rates, weight_f32, weight_sem)
    load_weights.start()

    barrier = pltpu.get_barrier_semaphore()
    pl.semaphore_signal(barrier, inc=1, device_id=at(a, b, other), device_id_type=MESH)
    for d in range(1, nb):
        pl.semaphore_signal(barrier, inc=1, device_id=at(a, b_plus(d), core), device_id_type=MESH)
    for d in range(1, na):
        pl.semaphore_signal(barrier, inc=1, device_id=at(lax.rem(a + d, na), b, core),
                            device_id_type=MESH)
    pl.semaphore_wait(barrier, 1 + (nb - 1) + (na - 1))

    def y_pre(c, d):
        return remote(pop.at[:, b_plus(d), :, pl.ds(c * width, width)], y_in.at[c, d - 1],
                      yp_s.at[c, d - 1], yp_r.at[c, d - 1], at(a, b_plus(d), core))

    def core_pre(c, e):
        if e == 0:
            src = pop.at[other, b, :, pl.ds(c * width, width)]
        else:
            src = y_in.at[c, e - 1, other]
        return remote(src, core_in.at[c, e], cp_s.at[c, e], cp_r.at[c, e], at(a, b, other))

    def start_y(c):
        for d in range(1, nb):
            y_pre(c, d).start()

    def turn(c):
        for d in range(1, nb):
            y_pre(c, d).wait_recv()
        for e in range(nb):
            core_pre(c, e).start()

    def assemble(c):
        for e in range(nb):
            core_pre(c, e).wait_recv()
        plane[c, b * 2 + core] = pop[core, b, :, c * width:(c + 1) * width]
        plane[c, b * 2 + other] = core_in[c, 0]
        for d in range(1, nb):
            plane[c, b_minus(d) * 2 + core] = y_in[c, d - 1, core]
            plane[c, b_minus(d) * 2 + other] = core_in[c, d]

    start_y(0)
    acc[...] = jnp.zeros_like(acc)
    turn(0)
    if chunks > 1:
        start_y(1)
    assemble(0)
    load_weights.wait()

    def up_copy(u):
        return remote(up.at[u], up.at[u], up_s.at[u], up_r.at[u], at(a + 1, b, core))

    def down_copy(u):
        return remote(down.at[u], down.at[u], dn_s.at[u], dn_r.at[u], at(a - 1, b, core))

    def y_post(u, d):
        return remote(full.at[u, core, b], full.at[u, core, b],
                      yq_s.at[u, d - 1], yq_r.at[u, d - 1], at(a, b_plus(d), core))

    def y_landed(u, d):
        here = full.at[u, core, b_minus(d)]
        return remote(here, here, yq_s.at[u, d - 1], yq_r.at[u, d - 1], at(a, b_minus(d), core))

    def core_post(u):
        return remote(full.at[u, core], full.at[u, core], cq_s.at[u], cq_r.at[u], at(a, b, other))

    def core_landed(u):
        return remote(full.at[u, other], full.at[u, other], cq_s.at[u], cq_r.at[u],
                      at(a, b, other))

    def flow(u, buffer, copy, first, last):
        k = lax.rem(u, panels)
        owner = owners[k]

        @pl.when(first)
        def _():
            buffer[u] = plane[u // panels, lax.rem(owner, 2 * nb)]

        @pl.when(jnp.logical_not(first))
        def _():
            copy(u).wait_recv()
            picked = plane[u // panels, lax.rem(owner, 2 * nb)]
            buffer[u] = jnp.where(owner // (2 * nb) == a, picked, buffer[u])

        @pl.when(jnp.logical_not(last))
        def _():
            copy(u).start()

    def prepare(k):
        def body(r, carry):
            for s in range(2):
                live = (s < counts[r, k]).astype(jnp.float32)
                hi, lo = split(weight_f32[r, k, s] * live)
                weights[k, r, 0:block_size, s * block_size:(s + 1) * block_size] = hi
                weights[k, r, block_size:2 * block_size,
                        s * block_size:(s + 1) * block_size] = lo
            return carry

        lax.fori_loop(0, block_rows, body, 0)

    def multiply(u):
        k = lax.rem(u, panels)
        c = u // panels

        @pl.when(u < panels)
        def _():
            prepare(k)

        hi, lo = split(full[u].reshape(block_rows, block_size, width))
        high[...] = hi
        low[...] = lo

        def body(r, carry):
            first, second = columns[r, k, 0], columns[r, k, 1]
            w = weights[k, r]
            p_hi = jnp.concatenate([high[first], high[second]], axis=0)
            p_lo = jnp.concatenate([low[first], low[second]], axis=0)
            both = jnp.dot(w, p_hi, preferred_element_type=jnp.float32)
            cross = jnp.dot(w[0:block_size], p_lo, preferred_element_type=jnp.float32)
            acc[c, r] += both[0:block_size] + (both[block_size:2 * block_size] + cross)
            return carry

        lax.fori_loop(0, block_rows, body, 0, unroll=True)

    def step(t, carry):
        for c in range(1, chunks):
            @pl.when(t == max(c * panels - 4, 0))
            def _():
                turn(c)
                if c + 1 < chunks:
                    start_y(c + 1)

            @pl.when(t == max(c * panels - 2, 0))
            def _():
                assemble(c)

        lag_up, lag_down = SKEW * a, SKEW * (na - 1 - a)
        u_up, u_down = t - lag_up, t - lag_down
        u_y = t - jnp.maximum(lag_up, lag_down)
        u_c = u_y - LAG_Y
        u_m = u_c - LAG_C

        @pl.when((u_up >= 0) & (u_up < units))
        def _():
            flow(u_up, up, up_copy, a == 0, a == na - 1)

        @pl.when((u_down >= 0) & (u_down < units))
        def _():
            flow(u_down, down, down_copy, a == na - 1, a == 0)

        @pl.when((u_y >= 0) & (u_y < units))
        def _():
            owner_a = owners[lax.rem(u_y, panels)] // (2 * nb)
            full[u_y, core, b] = jnp.where(owner_a <= a, up[u_y], down[u_y])
            for d in range(1, nb):
                y_post(u_y, d).start()

        @pl.when((u_c >= 0) & (u_c < units))
        def _():
            for d in range(1, nb):
                y_landed(u_c, d).wait_recv()
            core_post(u_c).start()

        @pl.when((u_m >= 0) & (u_m < units))
        def _():
            core_landed(u_m).wait_recv()
            multiply(u_m)

        return carry

    lax.fori_loop(0, units + SKEW * (na - 1) + LAG_Y + LAG_C, step, 0)

    for c in range(chunks):
        x = acc[c].reshape(block_rows * block_size // 8, 8, width)
        sum_mine[0, :, c * width:(c + 1) * width] = jnp.sum(x * x, axis=0)

    def sum_c():
        return remote(sum_mine.at[0], sum_core, sc_s, sc_r, at(a, b, other))

    def sum_b(d):
        return remote(sum_mine.at[1], sum_y.at[d - 1], sy_s.at[d - 1], sy_r.at[d - 1],
                      at(a, b_plus(d), core))

    def sum_over_a(d):
        return remote(sum_mine.at[2], sum_a.at[d - 1], sa_s.at[d - 1], sa_r.at[d - 1],
                      at(lax.rem(a + d, na), b, core))

    sum_c().start()
    for c in range(chunks):
        product[:, :, c * width:(c + 1) * width] = acc[c]
    sum_c().wait_recv()
    sum_mine[1] = sum_mine[0] + sum_core[...]
    for d in range(1, nb):
        sum_b(d).start()
    total = sum_mine[1]
    for d in range(1, nb):
        sum_b(d).wait_recv()
        total = total + sum_y[d - 1]
    sum_mine[2] = total
    for d in range(1, na):
        sum_over_a(d).start()
    for d in range(1, na):
        sum_over_a(d).wait_recv()
        total = total + sum_a[d - 1]
    squares[...] = total

    sum_c().wait_send()
    for d in range(1, nb):
        sum_b(d).wait_send()
    for d in range(1, na):
        sum_over_a(d).wait_send()
    for c in range(chunks):
        for d in range(1, nb):
            y_pre(c, d).wait_send()
        for e in range(nb):
            core_pre(c, e).wait_send()

    def drain(u, carry):
        @pl.when(a < na - 1)
        def _():
            up_copy(u).wait_send()

        @pl.when(a > 0)
        def _():
            down_copy(u).wait_send()

        for d in range(1, nb):
            y_post(u, d).wait_send()
        core_post(u).wait_send()
        return carry

    lax.fori_loop(0, units, drain, 0)


def on_device(devices, populations, rate_blocks, columns, counts, owners):
    block_rows, panels, slots, block_size, _ = rate_blocks.shape
    rows, chains = populations.shape
    na, nb = grid_of(devices)
    chunks = CHUNKS
    units = chunks * panels
    width = chains // chunks
    lane_rows = rows // (2 * nb)
    f32, bf16 = jnp.float32, jnp.bfloat16
    vmem = pl.BlockSpec(memory_space=pltpu.VMEM)
    smem = pl.BlockSpec(memory_space=pltpu.SMEM)
    dma = pltpu.SemaphoreType.DMA
    product, squares = pl.pallas_call(
        functools.partial(kernel, na, nb, chunks, panels),
        out_shape=(jax.ShapeDtypeStruct((block_rows, block_size, chains), f32),
                   jax.ShapeDtypeStruct((8, chains), f32)),
        in_specs=[vmem, pl.BlockSpec(memory_space=pl.ANY), smem, smem, smem],
        out_specs=(vmem, vmem),
        scratch_shapes=[
            pltpu.VMEM((block_rows, panels, slots, block_size, block_size), f32),
            pltpu.VMEM((panels, block_rows, 2 * block_size, slots * block_size), bf16),
            pltpu.VMEM((chunks, nb - 1, 2, lane_rows, width), f32),
            pltpu.VMEM((chunks, nb, lane_rows, width), f32),
            pltpu.VMEM((chunks, 2 * nb, lane_rows, width), f32),
            pltpu.VMEM((units, lane_rows, width), f32),
            pltpu.VMEM((units, lane_rows, width), f32),
            pltpu.VMEM((units, 2, nb, lane_rows, width), f32),
            pltpu.VMEM((block_rows, block_size, width), bf16),
            pltpu.VMEM((block_rows, block_size, width), bf16),
            pltpu.VMEM((chunks, block_rows, block_size, width), f32),
            pltpu.VMEM((3, 8, chains), f32),
            pltpu.VMEM((nb - 1, 8, chains), f32),
            pltpu.VMEM((8, chains), f32),
            pltpu.VMEM((na - 1, 8, chains), f32),
            dma,
            dma((chunks, nb - 1)), dma((chunks, nb - 1)),
            dma((chunks, nb)), dma((chunks, nb)),
            dma((units,)), dma((units,)),
            dma((units,)), dma((units,)),
            dma((units, nb - 1)), dma((units, nb - 1)),
            dma((units,)), dma((units,)),
            dma((nb - 1,)), dma((nb - 1,)),
            dma, dma,
            dma((na - 1,)), dma((na - 1,)),
        ],
        compiler_params=pltpu.CompilerParams(
            collective_id=0, has_side_effects=True, vmem_limit_bytes=56 * 1024 * 1024),
        cost_estimate=pl.CostEstimate(
            flops=6 * block_rows * panels * slots * block_size * block_size * chains,
            bytes_accessed=4 * (rate_blocks.size + 2 * populations.size), transcendentals=0),
    )(populations.reshape(2, nb, lane_rows, chains), rate_blocks, columns, counts, owners)
    chain_scale = jnp.sqrt(jnp.sum(squares, axis=0) / (rows * devices) + 1e-06)
    return product.reshape(rows, chains) / chain_scale, chain_scale


def solution(mesh):
    in_specs = (
        P(("grp", "row"), None),
        P(("grp", "row"), None, None, None, None),
        P(("grp", "row"), None, None),
        P(("grp", "row"), None),
        P(),
    )
    out_specs = (P(("grp", "row"), None), P("grp"))
    return jax.shard_map(
        functools.partial(on_device, mesh.shape["row"]),
        mesh=mesh, in_specs=in_specs, out_specs=out_specs, check_vma=False)
```

time: 385 us -> 125 us (0.32)
  waiting for transfers between devices: 238 us -> 0 us
  Pallas kernels: 0 us -> 118 us
  local copies, waits for them, and re-layouts: 44.8 us -> 1.42 us
  matrix products: 41.1 us -> 0 us
  blocking collectives: 31.8 us -> 0 us
  between operations: 18.3 us -> 0.65 us
  other arithmetic: 9.74 us -> 3.94 us
    psum x1 -> x0, waiting for transfers between devices: 238 us -> none  [spread(): return lax.psum(block, axis)]
    pallas_call x0 -> x1, Pallas kernels: none -> 118 us  [on_device(): pl.pallas_call(functools.partial(kernel, na, nb, chunks, panels), out_sha...]
    gather x12 -> x0, local copies, waits for them, and re-layouts: 42 us -> none  [on_device(): picked = contribute_panel_blocks[columns[:, k, contribute_s]]]
    dot_general x12 -> x0, matrix products: 41.1 us -> none  [on_device(): jnp.einsum('rij,rjc->ric', weight, picked, precision=lax.Precision.HIGHEST)]
    psum x1 -> x0, blocking collectives: 31.8 us -> none  [on_device(): total_squares = lax.psum(squares, 'row')]
    select_n x2 -> x0, other arithmetic: 6.47 us -> none  [the longest x1 6.46 us: spread(): jnp.where(lax.axis_index(axis) == holder, block, jnp.zeros_like(block))]
  transfers between devices with their start and end apart: 1 -> 0, of which waited for: 1 -> 0; matrix products, arithmetic and copies ran while one was open for 0% -> 0% of each run, Pallas kernels for 0% -> 0%
where the time goes in v1:
time: 125 us; the launch traced here: 124 us
  Pallas kernels  118 us (94%)
  other arithmetic  3.94 us (3%)
  local copies, waits for them, and re-layouts  1.42 us (1%)
    pallas_call x1, Pallas kernels, on_device(): pl.pallas_call(functools.partial(kernel, na, nb, chunks, panels), out_sha...  118 us
    div x1, other arithmetic, on_device(): return (product.reshape(rows, chains) / chain_scale, chain_scale)  3.19 us

profile of v1, /device:TPU:0, one launch (start us, length us, event | category | flops | bytes accessed | tf_op | source)
XLA Modules:
  0.0 124.4 jit_solution(14238012456169161027)
XLA Ops:
  0.6 1.4 %copy.7.columns = s32[8,6,2]{2,1,0:T(8,128)} copy(s32[8,6,2]{0,2,1:T(2,128)} %param.7) | data formatting | bytes 768 | tf_op args[2]
  2.0 118.4 %shard_map.68 = (f32[8,128,512]{2,1,0:T(8,128)}, f32[8,512]{1,0:T(8,128)}) custom-call(f32[2,2,256,512]{3,2,1,0:T(8,128)} %bitcast.3, f32[8,6,2,128,128]{4,3,2,1,0:T(8,128)} %rates.1, s32[8,6,2]{2,1,0:T(8,128)} %copy.7.columns, s32[8,6]{1,0:T(8,128)} %counts.1, s32[6]{0:T(128)} %owners.1), custom_call_target="tpu_custom_call" | custom-call | flops 4831838208 | bytes 10485760 | tf_op jit(solution)/shard_map/pallas_call | solution.py:306
  120.5 0.7 reduce_sum.9
  121.2 0.0 copy-start
  121.2 3.2 %bitcast_divide_fusion = f32[1024,512]{1,0:T(8,128)} fusion(f32[8,128,512]{2,1,0:T(8,128)} %get-tuple-element.4, f32[512]{0:T(512)S(1)} %add_sqrt_fusion), kind=kLoop, calls=%fused_computation | loop fusion | flops 524288 | bytes 4196352 | tf_op jit(solution)/shard_map/div | solution.py:346
  124.4 0.0 copy-done
  (1 shorter events, 0.0 us)
Async XLA Ops:
  121.2 3.2 %copy-start = (f32[512]{0:T(512)}, f32[512]{0:T(512)S(1)}, u32[]{:S(2)}) copy-start(f32[512]{0:T(512)S(1)} %add_sqrt_fusion) | copy-start | bytes 6148

commit v2 on v1

--- a/solution.py
+++ b/solution.py
@@ -8,9 +8,11 @@
 from jax.sharding import PartitionSpec as P
 
 CHUNKS = 4
+PIECES = 1
+THROTTLE = 0
 SKEW = 2
 LAG_Y = 2
-LAG_C = 1
+LAG_C = 2
 MESH = pl.DeviceIdType.MESH
 
 
@@ -28,7 +30,7 @@
     return high, low
 
 
-def kernel(na, nb, chunks, panels, pop, rates, columns, counts, owners, product, squares,
+def kernel(na, nb, chunks, pieces, panels, pop, rates, columns, counts, owners, product, squares,
            weight_f32, weights, y_in, core_in, plane, up, down, full, high, low, acc,
            sum_mine, sum_y, sum_core, sum_a, weight_sem,
            yp_s, yp_r, cp_s, cp_r, up_s, up_r, dn_s, dn_r, yq_s, yq_r, cq_s, cq_r,
@@ -38,8 +40,8 @@
     b = lax.rem(me // 2, nb)
     a = me // (2 * nb)
     other = 1 - core
-    units = chunks * panels
-    width = pop.shape[3] // chunks
+    units = chunks * panels * pieces
+    width = pop.shape[4] // chunks
     block_rows, block_size = product.shape[0], product.shape[1]
 
     def at(a_, b_, core_):
@@ -69,12 +71,12 @@
     pl.semaphore_wait(barrier, 1 + (nb - 1) + (na - 1))
 
     def y_pre(c, d):
-        return remote(pop.at[:, b_plus(d), :, pl.ds(c * width, width)], y_in.at[c, d - 1],
+        return remote(pop.at[:, b_plus(d), :, :, pl.ds(c * width, width)], y_in.at[c, d - 1],
                       yp_s.at[c, d - 1], yp_r.at[c, d - 1], at(a, b_plus(d), core))
 
     def core_pre(c, e):
         if e == 0:
-            src = pop.at[other, b, :, pl.ds(c * width, width)]
+            src = pop.at[other, b, :, :, pl.ds(c * width, width)]
         else:
             src = y_in.at[c, e - 1, other]
         return remote(src, core_in.at[c, e], cp_s.at[c, e], cp_r.at[c, e], at(a, b, other))
@@ -92,7 +94,7 @@
     def assemble(c):
         for e in range(nb):
             core_pre(c, e).wait_recv()
-        plane[c, b * 2 + core] = pop[core, b, :, c * width:(c + 1) * width]
+        plane[c, b * 2 + core] = pop[core, b, :, :, c * width:(c + 1) * width]
         plane[c, b * 2 + other] = core_in[c, 0]
         for d in range(1, nb):
             plane[c, b_minus(d) * 2 + core] = y_in[c, d - 1, core]
@@ -101,8 +103,8 @@
     start_y(0)
     acc[...] = jnp.zeros_like(acc)
     turn(0)
-    if chunks > 1:
-        start_y(1)
+    for c in range(1, chunks):
+        start_y(c)
     assemble(0)
     load_weights.wait()
 
@@ -113,36 +115,47 @@
         return remote(down.at[u], down.at[u], dn_s.at[u], dn_r.at[u], at(a - 1, b, core))
 
     def y_post(u, d):
-        return remote(full.at[u, core, b], full.at[u, core, b],
-                      yq_s.at[u, d - 1], yq_r.at[u, d - 1], at(a, b_plus(d), core))
+        here = full.at[u // pieces, core, b, lax.rem(u, pieces)]
+        return remote(here, here, yq_s.at[u, d - 1], yq_r.at[u, d - 1], at(a, b_plus(d), core))
 
     def y_landed(u, d):
-        here = full.at[u, core, b_minus(d)]
+        here = full.at[u // pieces, core, b_minus(d), lax.rem(u, pieces)]
         return remote(here, here, yq_s.at[u, d - 1], yq_r.at[u, d - 1], at(a, b_minus(d), core))
 
+    def core_copy(u, side):
+        here = full.at[u // pieces, side, :, lax.rem(u, pieces)]
+        return remote(here, here, cq_s.at[u], cq_r.at[u], at(a, b, other))
+
     def core_post(u):
-        return remote(full.at[u, core], full.at[u, core], cq_s.at[u], cq_r.at[u], at(a, b, other))
+        return core_copy(u, core)
 
     def core_landed(u):
-        return remote(full.at[u, other], full.at[u, other], cq_s.at[u], cq_r.at[u],
-                      at(a, b, other))
+        return core_copy(u, other)
+
+    def panel_of(u):
+        return lax.rem(u // pieces, panels)
 
     def flow(u, buffer, copy, first, last):
-        k = lax.rem(u, panels)
-        owner = owners[k]
+        owner = owners[panel_of(u)]
+
+        def picked():
+            return plane[u // (panels * pieces), lax.rem(owner, 2 * nb), lax.rem(u, pieces)]
 
         @pl.when(first)
         def _():
-            buffer[u] = plane[u // panels, lax.rem(owner, 2 * nb)]
+            buffer[u] = picked()
 
         @pl.when(jnp.logical_not(first))
         def _():
             copy(u).wait_recv()
-            picked = plane[u // panels, lax.rem(owner, 2 * nb)]
-            buffer[u] = jnp.where(owner // (2 * nb) == a, picked, buffer[u])
+            buffer[u] = jnp.where(owner // (2 * nb) == a, picked(), buffer[u])
 
         @pl.when(jnp.logical_not(last))
         def _():
+            if THROTTLE:
+                @pl.when(u >= THROTTLE)
+                def _():
+                    copy(u - THROTTLE).wait_send()
             copy(u).start()
 
     def prepare(k):
@@ -157,15 +170,15 @@
 
         lax.fori_loop(0, block_rows, body, 0)
 
-    def multiply(u):
-        k = lax.rem(u, panels)
-        c = u // panels
-
-        @pl.when(u < panels)
+    def multiply(m):
+        k = lax.rem(m, panels)
+        c = m // panels
+
+        @pl.when(m < panels)
         def _():
             prepare(k)
 
-        hi, lo = split(full[u].reshape(block_rows, block_size, width))
+        hi, lo = split(full[m].reshape(block_rows, block_size, width))
         high[...] = hi
         low[...] = lo
 
@@ -183,13 +196,11 @@
 
     def step(t, carry):
         for c in range(1, chunks):
-            @pl.when(t == max(c * panels - 4, 0))
+            @pl.when(t == max((c * panels - 4) * pieces, 0))
             def _():
                 turn(c)
-                if c + 1 < chunks:
-                    start_y(c + 1)
-
-            @pl.when(t == max(c * panels - 2, 0))
+
+            @pl.when(t == max((c * panels - 2) * pieces, 0))
             def _():
                 assemble(c)
 
@@ -209,8 +220,8 @@
 
         @pl.when((u_y >= 0) & (u_y < units))
         def _():
-            owner_a = owners[lax.rem(u_y, panels)] // (2 * nb)
-            full[u_y, core, b] = jnp.where(owner_a <= a, up[u_y], down[u_y])
+            owner_a = owners[panel_of(u_y)] // (2 * nb)
+            full[u_y // pieces, core, b, lax.rem(u_y, pieces)] = jnp.where(owner_a <= a, up[u_y], down[u_y])
             for d in range(1, nb):
                 y_post(u_y, d).start()
 
@@ -223,7 +234,10 @@
         @pl.when((u_m >= 0) & (u_m < units))
         def _():
             core_landed(u_m).wait_recv()
-            multiply(u_m)
+
+            @pl.when(lax.rem(u_m, pieces) == pieces - 1)
+            def _():
+                multiply(u_m // pieces)
 
         return carry
 
@@ -275,11 +289,13 @@
             core_pre(c, e).wait_send()
 
     def drain(u, carry):
-        @pl.when(a < na - 1)
+        left = u >= units - THROTTLE if THROTTLE else True
+
+        @pl.when((a < na - 1) & left)
         def _():
             up_copy(u).wait_send()
 
-        @pl.when(a > 0)
+        @pl.when((a > 0) & left)
         def _():
             down_copy(u).wait_send()
 
@@ -296,15 +312,16 @@
     rows, chains = populations.shape
     na, nb = grid_of(devices)
     chunks = CHUNKS
-    units = chunks * panels
+    pieces = PIECES
+    units = chunks * panels * pieces
     width = chains // chunks
-    lane_rows = rows // (2 * nb)
+    piece_rows = rows // (2 * nb * pieces)
     f32, bf16 = jnp.float32, jnp.bfloat16
     vmem = pl.BlockSpec(memory_space=pltpu.VMEM)
     smem = pl.BlockSpec(memory_space=pltpu.SMEM)
     dma = pltpu.SemaphoreType.DMA
     product, squares = pl.pallas_call(
-        functools.partial(kernel, na, nb, chunks, panels),
+        functools.partial(kernel, na, nb, chunks, pieces, panels),
         out_shape=(jax.ShapeDtypeStruct((block_rows, block_size, chains), f32),
                    jax.ShapeDtypeStruct((8, chains), f32)),
         in_specs=[vmem, pl.BlockSpec(memory_space=pl.ANY), smem, smem, smem],
@@ -312,12 +329,12 @@
         scratch_shapes=[
             pltpu.VMEM((block_rows, panels, slots, block_size, block_size), f32),
             pltpu.VMEM((panels, block_rows, 2 * block_size, slots * block_size), bf16),
-            pltpu.VMEM((chunks, nb - 1, 2, lane_rows, width), f32),
-            pltpu.VMEM((chunks, nb, lane_rows, width), f32),
-            pltpu.VMEM((chunks, 2 * nb, lane_rows, width), f32),
-            pltpu.VMEM((units, lane_rows, width), f32),
-            pltpu.VMEM((units, lane_rows, width), f32),
-            pltpu.VMEM((units, 2, nb, lane_rows, width), f32),
+            pltpu.VMEM((chunks, nb - 1, 2, pieces, piece_rows, width), f32),
+            pltpu.VMEM((chunks, nb, pieces, piece_rows, width), f32),
+            pltpu.VMEM((chunks, 2 * nb, pieces, piece_rows, width), f32),
+            pltpu.VMEM((units, piece_rows, width), f32),
+            pltpu.VMEM((units, piece_rows, width), f32),
+            pltpu.VMEM((chunks * panels, 2, nb, pieces, piece_rows, width), f32),
             pltpu.VMEM((block_rows, block_size, width), bf16),
             pltpu.VMEM((block_rows, block_size, width), bf16),
             pltpu.VMEM((chunks, block_rows, block_size, width), f32),
@@ -341,7 +358,7 @@
         cost_estimate=pl.CostEstimate(
             flops=6 * block_rows * panels * slots * block_size * block_size * chains,
             bytes_accessed=4 * (rate_blocks.size + 2 * populations.size), transcendentals=0),
-    )(populations.reshape(2, nb, lane_rows, chains), rate_blocks, columns, counts, owners)
+    )(populations.reshape(2, nb, pieces, piece_rows, chains), rate_blocks, columns, counts, owners)
     chain_scale = jnp.sqrt(jnp.sum(squares, axis=0) / (rows * devices) + 1e-06)
     return product.reshape(rows, chains) / chain_scale, chain_scale
 

time: 125 us -> 119 us (0.952)
  Pallas kernels: 118 us -> 113 us
    pallas_call x1, Pallas kernels: 118 us -> 113 us  [on_device(): pl.pallas_call(functools.partial(kernel, na, nb, chunks, pieces, panels),...]
where the time goes in v2:
time: 119 us
  Pallas kernels  113 us (95%)
  other arithmetic  3.94 us (3%)
  local copies, waits for them, and re-layouts  1.42 us (1%)
    pallas_call x1, Pallas kernels, on_device(): pl.pallas_call(functools.partial(kernel, na, nb, chunks, pieces, panels),...  113 us
    div x1, other arithmetic, on_device(): return (product.reshape(rows, chains) / chain_scale, chain_scale)  3.19 us

profile of v2, /device:TPU:0, one launch (start us, length us, event | category | flops | bytes accessed | tf_op | source)
XLA Modules:
  0.0 119.2 jit_solution(6263695072036697050)
XLA Ops:
  0.6 1.4 %copy.7.columns = s32[8,6,2]{2,1,0:T(8,128)} copy(s32[8,6,2]{0,2,1:T(2,128)} %param.7) | data formatting | bytes 768 | tf_op args[2]
  2.0 113.2 %shard_map.68 = (f32[8,128,512]{2,1,0:T(8,128)}, f32[8,512]{1,0:T(8,128)}) custom-call(f32[2,2,1,256,512]{4,3,2,1,0:T(8,128)} %bitcast.3, f32[8,6,2,128,128]{4,3,2,1,0:T(8,128)} %rates.1, s32[8,6,2]{2,1,0:T(8,128)} %copy.7.columns, s32[8,6]{1,0:T(8,128)} %counts.1, s32[6]{0:T(128)} %owners.1), custom_call_target="tpu_custom_call" | custom-call | flops 4831838208 | bytes 10485760 | tf_op jit(solution)/shard_map/pallas_call | solution.py:323
  115.2 0.7 reduce_sum.9
  116.0 0.0 copy-start
  116.0 3.2 %bitcast_divide_fusion = f32[1024,512]{1,0:T(8,128)} fusion(f32[8,128,512]{2,1,0:T(8,128)} %get-tuple-element.4, f32[512]{0:T(512)S(1)} %add_sqrt_fusion), kind=kLoop, calls=%fused_computation | loop fusion | flops 524288 | bytes 4196352 | tf_op jit(solution)/shard_map/div | solution.py:363
  119.2 0.0 copy-done
  (1 shorter events, 0.0 us)
Async XLA Ops:
  116.0 3.2 %copy-start = (f32[512]{0:T(512)}, f32[512]{0:T(512)S(1)}, u32[]{:S(2)}) copy-start(f32[512]{0:T(512)S(1)} %add_sqrt_fusion) | copy-start | bytes 6148
